TPU v7x, 32 devices: a whole 2x2x4 slice. The times are simulated.
32 devices in a mesh: groups: 2 (over y), curve: 4 (over z), mp: 4 (over x, core).
Axes of the slice: x: 2, y: 2, z: 4, core: 2. Of those that a mesh axis runs over, the one named last changes fastest.
Arguments:
- points: bfloat16 [8192, 512], P(('groups', 'curve')), parts along dimension 0, may hold values from -6 to 6
- owner: int32 [8192, 1], P(('groups', 'curve')), parts along dimension 0, may hold values from 0 to 3; in each aligned block of 1024 rows (0 to 1023, 1024 to 2047, ...) at most 512 rows name the same one
- local_order: int32 [8, 1024], P(('groups', 'curve')), parts along dimension 0, may hold values from 0 to 1023, each once within a row
- codes: int32 [8192], P(('groups', 'curve')), parts along dimension 0, may hold values from 1 to 4096
- w_in: bfloat16 [512, 4, 1024], P(None, None, 'mp'), may hold values from -0.25 to 0.25
- w_bc: bfloat16 [512, 4, 64], replicated, may hold values from -0.25 to 0.25
- decay_rate: float32 [2, 16], replicated, may hold values from 0 to 1
- dt_scale: float32 [2, 16], replicated, may hold values from 0.02 to 0.2
- skip_gain: float32 [2, 16], replicated, may hold values from 0.5 to 2
- w_out: bfloat16 [2, 1024, 512], replicated, may hold values from -0.125 to 0.125
Outputs:
- mixed: bfloat16 [8192, 512], P(('groups', 'curve'), 'mp'), parts along dimension 0
There are 2 independent parts, one for each index of `groups`. A program takes and returns all parts, laid end to end along the dimension named above; an argument that names none is the same for every part. Nothing has to cross between parts.
Inputs may be any that keep to these rules, and one draw needn't show every extreme that they name: Among the points of one device no owner is named by more than 512. `local_order`: each row lists the points of one device in curve order, each once.
All inputs are finite; a program needn't handle non-finite values.
Results may differ from a plain program's by a relative error of at most 0.02.
Values may be sent and summed in bfloat16 or wider, within the bound.
A program may use at most 128 MiB of HBM per device.

v0:
```python
import functools

import jax
import jax.numpy as jnp
from jax import lax
from jax.experimental import pallas as pl
from jax.experimental.pallas import tpu as pltpu
from jax.sharding import PartitionSpec as P

HEADS = 16
HEADDIM = 64
SPAN = 256
LOG2E = 1.4426950408889634
F32 = jnp.float32
BF16 = jnp.bfloat16
MESH = pl.DeviceIdType.MESH


def running(a, axis):
    size = a.shape[axis]
    lower = (jnp.arange(size)[:, None] >= jnp.arange(size)[None, :]).astype(F32)
    moved = jnp.tensordot(lower, a.astype(F32), axes=(1, axis), precision=lax.Precision.HIGHEST)
    return jnp.moveaxis(moved, 0, axis)


def prefix(value, axis, combine, identity, reverse):
    peers, place = (lax.axis_size(axis), lax.axis_index(axis))
    everything = jax.tree.map(
        lambda part, kind: lax.all_gather(part.astype(kind), axis),
        value,
        jax.tree.map(lambda a: jnp.bfloat16 if a.dtype == jnp.float32 else a.dtype, value),
    )
    start = jax.tree.map(
        lambda part, zero: jnp.broadcast_to(jnp.asarray(zero, part.dtype), part.shape),
        value,
        identity,
    )

    def lap(k, before):
        at = peers - 1 - k if reverse else k
        reached = at > place if reverse else at < place
        new = combine(
            before, jax.tree.map(lambda part, own: part[at].astype(own.dtype), everything, value)
        )
        return jax.tree.map(lambda a, b: jnp.where(reached, a, b), new, before)

    return lax.fori_loop(0, peers, lap, start)


def local_pass(inputs, keys, queries, logs):
    rows, heads_local, width = inputs.shape
    blocks = rows // SPAN
    xblock = inputs.reshape(blocks, SPAN, heads_local, width)
    kblock_low = keys.reshape(blocks, SPAN, keys.shape[1])
    qblock_low = queries.reshape(blocks, SPAN, queries.shape[1])
    kblock = kblock_low.astype(jnp.float32)
    qblock = qblock_low.astype(jnp.float32)
    lcum = running(logs.reshape(blocks, SPAN, heads_local), 1)
    scores = jnp.einsum("cqn,csn->cqs", qblock_low, kblock_low, preferred_element_type=jnp.float32)
    causal = jnp.arange(SPAN)[:, None] >= jnp.arange(SPAN)[None, :]
    gap = lcum[:, :, None, :] - lcum[:, None, :, :]
    weight = jnp.where(
        causal[None, :, :, None], jnp.exp(jnp.where(causal[None, :, :, None], gap, 0.0)), 0.0
    )
    intra = jnp.einsum(
        "cqsh,cshp->cqhp", scores[..., None] * weight, xblock, precision=lax.Precision.HIGHEST
    )
    tail = jnp.exp(lcum[:, -1:, :] - lcum)
    block_state = jnp.einsum(
        "csn,cshp->chnp", kblock, xblock * tail[..., None], precision=lax.Precision.HIGHEST
    )
    block_log = lcum[:, -1, :]

    def advance(state, item):
        log_c, new_state = item
        return (jnp.exp(log_c)[:, None, None] * state + new_state, state)

    start = jnp.zeros((heads_local, keys.shape[1], width), jnp.float32)
    final, entering = lax.scan(advance, start, (block_log, block_state))
    total_log = jnp.sum(block_log, axis=0)
    return ((qblock, lcum, intra, entering, block_log), (total_log, final))


def finish(pieces, carried):
    qblock, lcum, intra, entering, block_log = pieces
    before = running(block_log, 0) - block_log
    enter_all = entering + jnp.exp(before)[:, :, None, None] * carried[None]
    inter = jnp.exp(lcum)[..., None] * jnp.einsum(
        "cqn,chnp->cqhp", qblock, enter_all, precision=lax.Precision.HIGHEST
    )
    total = intra + inter
    return total.reshape(-1, total.shape[2], total.shape[3])


def combine(earlier, later):
    return (earlier[0] + later[0], jnp.exp(later[0])[:, None, None] * earlier[1] + later[1])


def per_device(
    points, owner, local_order, codes, w_in, w_bc, decay_rate, dt_scale, skip_gain, w_out
):
    n_curve = lax.axis_size("curve")
    n_model = lax.axis_size("mp")
    count = points.shape[0]
    rows = 2 * count
    slots = rows // n_curve
    heads_local = HEADS // n_model
    model_index = lax.axis_index("mp")
    order = local_order[0]
    sorted_owner = owner[:, 0][order]
    onehot = (sorted_owner[:, None] == jnp.arange(n_curve, dtype=jnp.int32)[None, :]).astype(
        jnp.int32
    )
    slot = jnp.sum(running(onehot, 0) * onehot, axis=1).astype(jnp.int32) - 1
    target = jnp.zeros((count,), jnp.int32).at[order].set(sorted_owner * slots + slot)
    send_codes = jnp.zeros((rows,), jnp.int32).at[target].set(codes)
    send_rows = jnp.zeros((rows, points.shape[1]), points.dtype).at[target].set(points)
    arrived, arrived_codes = (
        lax.all_to_all(send_rows, "curve", split_axis=0, concat_axis=0, tiled=True),
        lax.all_to_all(send_codes, "curve", split_axis=0, concat_axis=0, tiled=True),
    )
    proj_sum = jnp.einsum("rk,kjc->rjc", arrived, w_in, preferred_element_type=jnp.float32)
    bc_sum = jnp.einsum("rk,kjc->rjc", arrived, w_bc, preferred_element_type=jnp.float32)
    proj = lax.optimization_barrier(proj_sum.astype(jnp.bfloat16)).astype(jnp.float32)
    bc = bc_sum.astype(jnp.bfloat16)
    code_f = arrived_codes.astype(jnp.float32)
    rates = lax.dynamic_slice_in_dim(decay_rate, model_index * heads_local, heads_local, 1)
    steps_dt = lax.dynamic_slice_in_dim(dt_scale, model_index * heads_local, heads_local, 1)
    skips = lax.dynamic_slice_in_dim(skip_gain, model_index * heads_local, heads_local, 1)
    pieces = []
    summaries = []
    xparts = []
    gates = []
    for direction in range(2):
        xh = proj[:, 2 * direction].reshape(rows, heads_local, HEADDIM)
        gates.append(proj[:, 2 * direction + 1].reshape(rows, heads_local, HEADDIM))
        xparts.append(xh)
        inputs = xh * steps_dt[direction][None, :, None]
        keys = bc[:, 2 * direction]
        queries = bc[:, 2 * direction + 1]
        logs = -rates[direction][None, :] * code_f[:, None]
        if direction == 1:
            inputs, keys, queries, logs = (
                jnp.flip(inputs, 0),
                jnp.flip(keys, 0),
                jnp.flip(queries, 0),
                jnp.flip(logs, 0),
            )
        kept, summary = local_pass(inputs, keys, queries, logs)
        pieces.append(kept)
        summaries.append(summary)
    ident = (jnp.zeros((heads_local,), jnp.float32), jnp.zeros_like(summaries[0][1]))
    forward_in = prefix(summaries[0], "curve", combine, ident, False)[1]
    backward_in = prefix(summaries[1], "curve", combine, ident, True)[1]
    carried_all = (forward_in, backward_in)
    normed = []
    for direction in range(2):
        outs = finish(pieces[direction], carried_all[direction])
        if direction == 1:
            outs = jnp.flip(outs, 0)
        outs = outs + skips[direction][None, :, None] * xparts[direction]
        value = outs * jax.nn.silu(gates[direction])
        value = value / jnp.sqrt(jnp.mean(value * value, axis=-1, keepdims=True) + 1e-05)
        normed.append(value.astype(jnp.bfloat16).reshape(rows, heads_local * HEADDIM))
    stacked = jnp.stack(normed, axis=1)
    w_rows = lax.dynamic_slice_in_dim(
        w_out, model_index * heads_local * HEADDIM, heads_local * HEADDIM, 1
    )
    terms = jnp.einsum("rdk,dkc->rc", stacked, w_rows, preferred_element_type=jnp.float32)
    summed = lax.psum_scatter(terms.astype(jnp.bfloat16), "mp", scatter_dimension=1, tiled=True)
    back = lax.all_to_all(summed, "curve", split_axis=0, concat_axis=0, tiled=True)
    return back[target]


def mm(a, b, ca=1, cb=0):
    return lax.dot_general(a, b, (((ca,), (cb,)), ((), ())), preferred_element_type=F32)


def iota(shape, dim):
    return lax.broadcasted_iota(jnp.int32, shape, dim)


def as_bf16(mask):
    return jnp.where(mask, 1.0, 0.0).astype(BF16)


def layer_kernel(
    nc,
    slots,
    pts,
    own,
    order,
    codes,
    w,
    rate_lane,
    dt_lane,
    skip_lane,
    rate,
    wo,
    out,
    sendb,
    tt,
    csend,
    carr,
    arr,
    proj,
    cols,
    rowv,
    ctot,
    cst,
    ent,
    pre,
    ssend,
    srecv,
    dsend,
    drecv,
    carried,
    part,
    recva,
    sendx,
    recvx,
    sumc,
    back,
    zs,
    zr,
    cs,
    cr,
    xs,
    xr,
    ps,
    pr,
    fs,
    fr,
    ss,
    sr,
    ds,
    dr,
    gs,
    gr,
    hs,
    hr,
    bs,
    br,
):
    count = pts.shape[0]
    share = slots // 4
    halves = slots // SPAN
    chunks = nc * halves
    me = lax.axis_index("curve")
    q = lax.axis_index("mp")
    core = lax.rem(q, 2)
    xx = lax.div(q, 2)
    other_core = q + 1 - 2 * core
    other_x = q + 2 - 4 * xx
    to_core = {"mp": other_core}
    to_x = {"mp": other_x}

    def after(k):
        return lax.rem(me + k, nc)

    def before(k):
        return lax.rem(me - k + nc, nc)

    def copy(src, dst, s, r, where):
        return pltpu.make_async_remote_copy(
            src_ref=src, dst_ref=dst, send_sem=s, recv_sem=r, device_id=where, device_id_type=MESH
        )

    def at(start, size):
        return pl.ds(pl.multiple_of(start, size), size)

    barrier = pltpu.get_barrier_semaphore()
    for k in range(1, nc):
        pl.semaphore_signal(barrier, inc=1, device_id={"curve": after(k)}, device_id_type=MESH)
    for there in (to_core, to_x):
        pl.semaphore_signal(barrier, inc=1, device_id=there, device_id_type=MESH)

    picks = as_bf16(iota((count, count), 0) == order[...])
    own8 = jnp.broadcast_to(own[...].astype(F32), (8, count)).astype(BF16)
    sorted8 = mm(own8, picks)
    hot8 = as_bf16(sorted8 == iota((8, count), 0).astype(F32))
    upper = as_bf16(iota((count, count), 0) <= iota((count, count), 1))
    counts = mm(hot8, upper)
    slot = jnp.sum(counts * hot8.astype(F32), axis=0, keepdims=True) - 1.0
    target = sorted8[0:1] * float(slots) + slot
    high = jnp.floor(target * (1.0 / 64.0))
    low = target - high * 64.0
    split8 = jnp.where(iota((8, count), 0) == 0, high, low).astype(BF16)
    trow8 = mm(split8, picks, 1, 1)
    trow = trow8[0:1] * 64.0 + trow8[1:2]
    tcol8 = mm(picks, split8, 1, 1)
    tcol = tcol8[:, 0:1] * 64.0 + tcol8[:, 1:2]

    def routed(t):
        place = (iota((share, count), 0) + (t * slots + q * share)).astype(F32)
        return mm(as_bf16(place == trow), pts[...]).astype(BF16)

    def zcopy(k):
        return copy(
            sendb.at[k],
            arr.at[at(me * slots + q * share, share)],
            zs.at[k],
            zr.at[k],
            {"curve": after(k)},
        )

    def ccopy(k):
        return copy(csend.at[after(k)], carr.at[me], cs.at[k], cr.at[k], {"curve": after(k)})

    def mine(s, who):
        return arr.at[at(s * slots + who * share, share)]

    def xcopy(k):
        s = before(k)
        return copy(mine(s, q), mine(s, q), xs.at[k], xr.at[k], to_x)

    def pcopy(k):
        s = before(k)
        return copy(mine(s, q), mine(s, q), ps.at[k], pr.at[k], to_core)

    def fcopy(k):
        s = before(k)
        return copy(mine(s, other_x), mine(s, other_x), fs.at[k], fr.at[k], to_core)

    first = routed(after(nc - 1))
    sendb[nc - 1] = first
    pl.semaphore_wait(barrier, nc + 1)
    zcopy(nc - 1).start()
    for k in range(nc - 2, 0, -1):
        sendb[k] = routed(after(k))
        zcopy(k).start()
    arr[at(me * slots + q * share, share)] = routed(me)
    xcopy(0).start()
    pcopy(0).start()

    codef = codes[...].astype(F32)
    chigh = jnp.floor(codef * (1.0 / 128.0))
    code8 = jnp.where(iota((8, count), 0) == 0, chigh, codef - chigh * 128.0).astype(BF16)
    for t in range(nc):
        hot = as_bf16(tcol == (iota((count, slots), 1) + t * slots).astype(F32))
        tt[t] = hot
        made = mm(code8, hot)
        for h in range(halves):
            csend[t, h] = made[:, h * SPAN : (h + 1) * SPAN]
    for k in range(1, nc):
        ccopy(k).start()
    carr[me] = csend[me]

    above = iota((SPAN, SPAN), 0) <= iota((SPAN, SPAN), 1)
    below = iota((SPAN, SPAN), 0) >= iota((SPAN, SPAN), 1)

    def project(s):
        def half(h, _):
            c = s * halves + h
            rows = at(c * SPAN, SPAN)
            made = mm(arr[rows, :], w[...]).astype(BF16)
            proj[rows, :] = made
            c8 = carr[s, h].astype(BF16)
            run8 = mm(c8, as_bf16(above))
            srow = run8[0:1] * 128.0 + run8[1:2]
            own_row = carr[s, h]
            erow = srow - (own_row[0:1] * 128.0 + own_row[1:2])
            rowv[c, 0:1, :] = srow
            rowv[c, 1:2, :] = erow
            scol8 = mm(as_bf16(below), c8, 1, 1)
            scol = scol8[:, 0:1] * 128.0 + scol8[:, 1:2]
            strict = as_bf16(iota((SPAN, SPAN), 0) > iota((SPAN, SPAN), 1))
            ecol8 = mm(strict, c8, 1, 1)
            ecol = ecol8[:, 0:1] * 128.0 + ecol8[:, 1:2]
            cols[0, rows, :] = jnp.broadcast_to(scol, (SPAN, 128))
            cols[1, rows, :] = jnp.broadcast_to(ecol, (SPAN, 128))
            total = srow[:, SPAN - 1 : SPAN]
            ctot[c] = jnp.broadcast_to(total, (8, 256))
            for d, reach in ((0, scol - total), (1, -ecol)):
                tail = jnp.exp2(rate_lane[d] * reach)
                xt = (made[:, 512 * d : 512 * d + 256].astype(F32) * tail).astype(BF16)
                keys = made[:, 1024 + 256 * d : 1152 + 256 * d]
                cst[d, c] = mm(keys, xt, 0, 0)[0:64]
            return 0

        lax.fori_loop(0, halves, half, 0)

    def complete(k):
        pcopy(k).wait_recv()
        fcopy(k).wait_recv()
        if k:
            ccopy(k).wait_recv()
        project(before(k))

    xcopy(0).wait_recv()
    fcopy(0).start()
    for k in range(1, nc):
        zcopy(k).wait_recv()
        xcopy(k).start()
        pcopy(k).start()
        complete(k - 1)
        xcopy(k).wait_recv()
        fcopy(k).start()
    complete(nc - 1)

    for d in range(2):
        state = jnp.zeros((64, 256), F32)
        passed = jnp.zeros((8, 256), F32)
        for step in range(chunks):
            c = step if d == 0 else chunks - 1 - step
            ent[d, c] = state
            pre[d, c] = passed
            gone = ctot[c]
            state = jnp.exp2(-rate_lane[d] * gone[0:1]) * state + cst[d, c]
            passed = passed + gone
        ssend[d] = state.astype(BF16)
        dsend[...] = passed

    def scopy(k):
        t = after(k)
        which = jnp.where(t > me, 0, 1)
        return copy(ssend.at[which], srecv.at[k], ss.at[k], sr.at[k], {"curve": t})

    def dcopy(k):
        return copy(dsend, drecv.at[k], ds.at[k], dr.at[k], {"curve": after(k)})

    for k in range(1, nc):
        scopy(k).start()
        dcopy(k).start()
    for k in range(1, nc):
        scopy(k).wait_recv()
        dcopy(k).wait_recv()
    for d in range(2):
        total = jnp.zeros((64, 256), F32)
        for k in range(1, nc):
            s = before(k)
            gap = jnp.zeros((1, 256), F32)
            for j in range(1, nc):
                u = before(j)
                if d == 0:
                    inside = jnp.logical_and(u > s, u < me)
                else:
                    inside = jnp.logical_and(u < s, u > me)
                gap = gap + jnp.where(inside, drecv[j][0:1], 0.0)
            counted = (s < me) if d == 0 else (s > me)
            term = jnp.exp2(-rate_lane[d] * gap) * srecv[k].astype(F32)
            total = total + jnp.where(counted, term, 0.0)
        carried[d] = total

    def attend(c):
        rows = at(c * SPAN, SPAN)
        normed = []
        for d in range(2):
            x = proj[rows, 512 * d : 512 * d + 256]
            z = proj[rows, 512 * d + 256 : 512 * d + 512].astype(F32)
            keys = proj[rows, 1024 + 256 * d : 1152 + 256 * d]
            queries = proj[rows, 1152 + 256 * d : 1280 + 256 * d]
            scores = jnp.where(below if d == 0 else above, mm(queries, keys, 1, 1), 0.0)
            col = cols[d, rows, :]
            col = jnp.concatenate([col, col], axis=1)
            row = rowv[c, d : d + 1, :]
            gap = jnp.minimum((row - col) if d == 0 else (col - row), 0.0)
            pairs = []
            for p in range(2):
                xp = x[:, 128 * p : 128 * p + 128]
                left = iota((SPAN, 128), 1) < 64
                nothing = jnp.zeros_like(xp)
                weights = [
                    (scores * jnp.exp2(rate[d, 2 * p + h] * gap)).astype(BF16) for h in range(2)
                ]
                pairs.append(
                    mm(
                        jnp.concatenate(weights, axis=1),
                        jnp.concatenate(
                            [jnp.where(left, xp, nothing), jnp.where(left, nothing, xp)], axis=0
                        ),
                    )
                )
            intra = jnp.concatenate(pairs, axis=1)
            lanes = rate_lane[d]
            entering = ent[d, c] + jnp.exp2(-lanes * pre[d, c][0:1]) * carried[d]
            reach = -col if d == 0 else col - ctot[c][0:1]
            inter = mm(queries[:, 0:64], entering.astype(BF16)) * jnp.exp2(lanes * reach)
            y = dt_lane[d] * (intra + inter) + skip_lane[d] * x.astype(F32)
            v = y * (z / (1.0 + jnp.exp(-z)))
            same = as_bf16((iota((256, 256), 0) // 64) == (iota((256, 256), 1) // 64))
            mean = mm((v * v).astype(BF16), same) * (1.0 / 64.0)
            normed.append((v * lax.rsqrt(mean + 1e-05)).astype(BF16))
        terms = mm(jnp.concatenate(normed, axis=1), wo[...]).astype(BF16)
        for m in range(4):
            part[m % 2, m // 2, rows, :] = terms[:, 128 * m : 128 * m + 128]

    def rows_of(k):
        return at(after(k) * slots, slots)

    def acopy(k):
        rows = rows_of(k)
        return copy(part.at[1 - core, :, rows], recva.at[:, rows], gs.at[k], gr.at[k], to_core)

    def bcopy(k):
        rows = rows_of(k)
        return copy(sendx.at[rows], recvx.at[rows], hs.at[k], hr.at[k], to_x)

    def backcopy(k):
        return copy(
            sumc.at[rows_of(k)], back.at[at(me * slots, slots)], bs.at[k], br.at[k], {"curve": after(k)}
        )

    def cross(k):
        acopy(k).wait_recv()
        rows = rows_of(k)
        sendx[rows, :] = (
            part[core, 1 - xx, rows, :].astype(F32) + recva[1 - xx, rows, :].astype(F32)
        ).astype(BF16)
        bcopy(k).start()

    def home(k):
        bcopy(k).wait_recv()
        rows = rows_of(k)
        total = (
            part[core, xx, rows, :].astype(F32)
            + recva[xx, rows, :].astype(F32)
            + recvx[rows, :].astype(F32)
        ).astype(BF16)
        if k:
            sumc[rows, :] = total
            backcopy(k).start()
        else:
            back[rows, :] = total

    turns = list(range(nc - 1, -1, -1))
    for step in range(nc + 2):
        if step < nc:
            k = turns[step]

            def one(h, _, k=k):
                attend(after(k) * halves + h)
                return 0

            lax.fori_loop(0, halves, one, 0)
            acopy(k).start()
        if 1 <= step <= nc:
            cross(turns[step - 1])
        if 2 <= step:
            home(turns[step - 2])
    for k in range(1, nc):
        backcopy(k).wait_recv()
    total = jnp.zeros((count, 128), F32)
    for t in range(nc):
        total = total + mm(tt[t], back[t * slots : (t + 1) * slots, :])
    out[...] = total.astype(BF16)

    for k in range(nc):
        xcopy(k).wait_send()
        pcopy(k).wait_send()
        fcopy(k).wait_send()
        acopy(k).wait_send()
        bcopy(k).wait_send()
        if k:
            zcopy(k).wait_send()
            ccopy(k).wait_send()
            scopy(k).wait_send()
            dcopy(k).wait_send()
            backcopy(k).wait_send()


def fused_device(
    points, owner, local_order, codes, w_in, w_bc, decay_rate, dt_scale, skip_gain, w_out
):
    nc = lax.axis_size("curve")
    n_model = lax.axis_size("mp")
    count, width = points.shape
    rows = 2 * count
    slots = rows // nc
    halves = slots // SPAN
    chunks = nc * halves
    hl = HEADS // n_model
    cut = hl * HEADDIM
    m = lax.axis_index("mp")
    rates = lax.dynamic_slice_in_dim(decay_rate, m * hl, hl, 1) * LOG2E
    steps = lax.dynamic_slice_in_dim(dt_scale, m * hl, hl, 1)
    skips = lax.dynamic_slice_in_dim(skip_gain, m * hl, hl, 1)
    lanes = lambda a: jnp.repeat(a, HEADDIM, axis=1)[:, None, :]
    wbc = jnp.pad(w_bc, ((0, 0), (0, 0), (0, 64))).reshape(width, 512)
    w = jnp.concatenate([w_in.reshape(width, 4 * cut), wbc], axis=1)
    wo = lax.dynamic_slice_in_dim(w_out, m * cut, cut, 1).reshape(2 * cut, width)
    vm = pltpu.VMEM
    sem = pltpu.SemaphoreType.DMA
    vspec = pl.BlockSpec(memory_space=pltpu.VMEM)
    sspec = pl.BlockSpec(memory_space=pltpu.SMEM)
    return pl.pallas_call(
        functools.partial(layer_kernel, nc, slots),
        out_shape=jax.ShapeDtypeStruct((count, width // 4), BF16),
        in_specs=[vspec] * 8 + [sspec, vspec],
        out_specs=vspec,
        scratch_shapes=[
            vm((nc, slots // 4, width), BF16),
            vm((nc, count, slots), BF16),
            vm((nc, halves, 8, SPAN), F32),
            vm((nc, halves, 8, SPAN), F32),
            vm((rows, width), BF16),
            vm((rows, w.shape[1]), BF16),
            vm((2, rows, 128), F32),
            vm((chunks, 8, SPAN), F32),
            vm((chunks, 8, 256), F32),
            vm((2, chunks, 64, 256), F32),
            vm((2, chunks, 64, 256), F32),
            vm((2, chunks, 8, 256), F32),
            vm((2, 64, 256), BF16),
            vm((nc, 64, 256), BF16),
            vm((8, 256), F32),
            vm((nc, 8, 256), F32),
            vm((2, 64, 256), F32),
            vm((2, 2, rows, 128), BF16),
            vm((2, rows, 128), BF16),
            vm((rows, 128), BF16),
            vm((rows, 128), BF16),
            vm((rows, 128), BF16),
            vm((rows, 128), BF16),
        ]
        + [sem((nc,))] * 20,
        compiler_params=pltpu.CompilerParams(
            collective_id=0, has_side_effects=True, vmem_limit_bytes=56 * 1024 * 1024
        ),
    )(
        points,
        owner.reshape(1, count),
        local_order,
        codes.reshape(1, count),
        w,
        lanes(rates),
        lanes(steps),
        lanes(skips),
        rates,
        wo,
    )


def solution(mesh):
    placed = (
        P(("groups", "curve"), None),
        P(("groups", "curve"), None),
        P(("groups", "curve"), None),
        P(("groups", "curve")),
        P(None, None, "mp"),
        P(),
        P(),
        P(),
        P(),
        P(),
    )
    sizes = dict(mesh.shape)

    def body(points, *rest):
        slots = 2 * points.shape[0] // sizes["curve"]
        if sizes["mp"] == 4 and slots % SPAN == 0 and sizes["curve"] <= 8:
            return fused_device(points, *rest)
        return per_device(points, *rest)

    return jax.shard_map(
        body,
        mesh=mesh,
        in_specs=placed,
        out_specs=P(("groups", "curve"), "mp"),
        check_vma=False,
    )
```

profile of v0, /device:TPU:0, one launch (start us, length us, event | category | flops | bytes accessed | tf_op | source)
XLA Modules:
  0.0 74.6 jit_solution(13733524025990463211)
XLA Ops:
  0.0 0.0 copy-start
  0.0 1.1 %pad.4 = bf16[512,4,128]{0,2,1:T(8,128)(2,1)S(1)} pad(bf16[512,4,64]{0,2,1:T(8,128)(2,1)} %param.15, bf16[]{:T(256)} %constant.2.clone.1), padding=0_0x0_0x0_64 | pad | bytes 786434 | tf_op jit(solution)/shard_map/jit(_pad)/pad | solution.py:579
  1.1 0.2 copy.12
  1.4 1.4 %copy.13 = bf16[64,8,4,256]{3,1,2,0:T(8,128)(2,1)S(1)} copy(bf16[64,8,4,256]{3,2,1,0:T(4,128)(2,1)} %bitcast.9) | data formatting | bytes 2097152
  2.8 0.0 copy-start.3
  2.8 0.0 copy-start.4
  2.8 0.0 copy-start.2
  2.9 1.3 %pad_maximum_fusion.w = bf16[512,1536]{1,0:T(8,128)(2,1)} fusion(bf16[512,512]{1,0:T(8,128)(2,1)S(1)} %copy.12, bf16[512,1024]{1,0:T(8,128)(2,1)S(1)} %bitcast.6), kind=kLoop, calls=%fused_computation | loop fusion | flops 3145728 | bytes 3145728 | tf_op jit(solution)/shard_map/concatenate | solution.py:580
  4.1 0.0 copy-done.3
  4.1 0.0 copy-done.4
  4.1 0.1 dynamic-slice_multiply_fusion
  4.2 0.1 broadcast_in_dim.9
  4.3 0.7 broadcast_in_dim_reshape.9.rate_lane
  4.9 0.0 copy-done.2
  4.9 0.1 constant_dynamic-slice_fusion.2
  5.0 0.1 broadcast_in_dim.10
  5.1 0.7 broadcast_in_dim_reshape.10.dt_lane
  5.7 0.1 broadcast_in_dim.11
  5.8 0.6 broadcast_in_dim_reshape.11.skip_lane
  6.5 0.0 copy-done
  6.5 0.8 %constant_dynamic-slice_fusion = bf16[2,256,512]{2,1,0:T(8,128)(2,1)} fusion(bf16[2,1024,512]{2,1,0:T(8,128)(2,1)S(1)} %copy-done, s32[]{:T(128)S(6)} %select_n.9), kind=kLoop, calls=%fused_computation.2 | loop fusion | bytes 1048580 | tf_op jit(solution)/shard_map/dynamic_slice | solution.py:581
  7.3 0.0 copy-done.1
  7.3 65.7 %shard_map.100 = bf16[1024,128]{1,0:T(8,128)(2,1)} custom-call(bf16[1024,512]{1,0:T(8,128)(2,1)} %pts.1, s32[1,1024]{1,0:T(1,128)} %bitcast.10, s32[1,1024]{1,0:T(1,128)} %order.1, s32[1,1024]{1,0:T(1,128)} %bitcast.11, bf16[512,1536]{1,0:T(8,128)(2,1)} %pad_maximum_fusion.w, f32[2,1,256]{2,1,0:T(1,128)} %broadcast_in_dim_reshape.9.rate_lane, ...), custom_call_target="tpu_custom_call" | custom-call | tf_op jit(solution)/shard_map/pallas_call | solution.py:586
  73.0 1.7 %copy.15 = bf16[1024,128]{1,0:T(8,128)(2,1)} copy(bf16[1024,128]{1,0:T(8,128)(2,1)} %shard_map.100) | data formatting | bytes 524288
  (1 shorter events, 0.0 us)
Async XLA Ops:
  0.0 6.5 %copy-start = (bf16[2,1024,512]{2,1,0:T(8,128)(2,1)S(1)}, bf16[2,1024,512]{2,1,0:T(8,128)(2,1)}, u32[]{:S(2)}) copy-start(bf16[2,1024,512]{2,1,0:T(8,128)(2,1)} %param.19) | copy-start | bytes 6291460
  2.8 1.3 %copy-start.3 = (f32[2,16]{1,0:T(2,128)S(1)}, f32[2,16]{1,0:T(2,128)}, u32[]{:S(2)}) copy-start(f32[2,16]{1,0:T(2,128)} %param.16) | copy-start | bytes 388
  2.8 1.3 %copy-start.4 = (f32[2,16]{1,0:T(2,128)S(1)}, f32[2,16]{1,0:T(2,128)}, u32[]{:S(2)}) copy-start(f32[2,16]{1,0:T(2,128)} %param.18) | copy-start | bytes 388
  2.8 2.1 %copy-start.2 = (f32[2,16]{1,0:T(2,128)S(1)}, f32[2,16]{1,0:T(2,128)}, u32[]{:S(2)}) copy-start(f32[2,16]{1,0:T(2,128)} %param.17) | copy-start | bytes 388
  4.2 3.1 %copy-start.1 = (f32[2,4]{1,0:T(2,128)}, f32[2,4]{1,0:T(2,128)S(1)}, u32[]{:S(2)}) copy-start(f32[2,4]{1,0:T(2,128)S(1)} %get-tuple-element.5.rate) | copy-start | bytes 100
where the time goes:
time: 74.8 us; the launch traced here: 74.6 us
  Pallas kernels  65.7 us (88%)
  local copies, waits for them, and re-layouts  7.57 us (10%)
  other arithmetic  1.33 us (2%)
    pallas_call x1, Pallas kernels, fused_device(): pl.pallas_call(functools.partial(layer_kernel, nc, slots), out_shape=jax....  65.7 us
    unnamed x12, local copies, waits for them, and re-layouts  3.14 us
    another operation x3, local copies, waits for them, and re-layouts, fused_device(): lanes = lambda a: jnp.repeat(a, HEADDIM, axis=1)[:, None, :]  1.97 us

commit v1 on v0

--- a/solution.py
+++ b/solution.py
@@ -191,13 +191,16 @@
     own,
     order,
     codes,
+    w_in,
+    w_bc,
+    rate,
+    dt,
+    skip,
+    w_out,
+    out,
     w,
-    rate_lane,
-    dt_lane,
-    skip_lane,
-    rate,
     wo,
-    out,
+    wsem,
     sendb,
     tt,
     csend,
@@ -205,7 +208,7 @@
     arr,
     proj,
     cols,
-    rowv,
+    yin,
     ctot,
     cst,
     ent,
@@ -269,6 +272,24 @@
     def at(start, size):
         return pl.ds(pl.multiple_of(start, size), size)
 
+    loads = [
+        pltpu.make_async_copy(w_in, w.at[:, 0:1024], wsem.at[0]),
+        pltpu.make_async_copy(w_out.at[:, at(q * 256, 256), :], wo, wsem.at[1]),
+    ]
+    for load in loads:
+        load.start()
+
+    def lane_values(table, d):
+        head = iota((1, 256), 1) // HEADDIM
+        made = jnp.full((1, 256), table[d, q * 4], F32)
+        for h in range(1, 4):
+            made = jnp.where(head == h, table[d, q * 4 + h], made)
+        return made
+
+    rate_lane = [lane_values(rate, d) * LOG2E for d in range(2)]
+    dt_lane = [lane_values(dt, d) for d in range(2)]
+    skip_lane = [lane_values(skip, d) for d in range(2)]
+
     barrier = pltpu.get_barrier_semaphore()
     for k in range(1, nc):
         pl.semaphore_signal(barrier, inc=1, device_id={"curve": after(k)}, device_id_type=MESH)
@@ -346,6 +367,13 @@
         ccopy(k).start()
     carr[me] = csend[me]
 
+    for j in range(4):
+        w[:, 1024 + 128 * j : 1152 + 128 * j] = jnp.concatenate(
+            [w_bc[:, 64 * j : 64 * j + 64], jnp.zeros((w_bc.shape[0], 64), BF16)], axis=1
+        )
+    for load in loads:
+        load.wait()
+
     above = iota((SPAN, SPAN), 0) <= iota((SPAN, SPAN), 1)
     below = iota((SPAN, SPAN), 0) >= iota((SPAN, SPAN), 1)
 
@@ -360,8 +388,6 @@
             srow = run8[0:1] * 128.0 + run8[1:2]
             own_row = carr[s, h]
             erow = srow - (own_row[0:1] * 128.0 + own_row[1:2])
-            rowv[c, 0:1, :] = srow
-            rowv[c, 1:2, :] = erow
             scol8 = mm(as_bf16(below), c8, 1, 1)
             scol = scol8[:, 0:1] * 128.0 + scol8[:, 1:2]
             strict = as_bf16(iota((SPAN, SPAN), 0) > iota((SPAN, SPAN), 1))
@@ -376,6 +402,26 @@
                 xt = (made[:, 512 * d : 512 * d + 256].astype(F32) * tail).astype(BF16)
                 keys = made[:, 1024 + 256 * d : 1152 + 256 * d]
                 cst[d, c] = mm(keys, xt, 0, 0)[0:64]
+            for d in range(2):
+                x = made[:, 512 * d : 512 * d + 256]
+                keys = made[:, 1024 + 256 * d : 1152 + 256 * d]
+                queries = made[:, 1152 + 256 * d : 1280 + 256 * d]
+                scores = jnp.where(below if d == 0 else above, mm(queries, keys, 1, 1), 0.0)
+                gap = jnp.minimum((srow - scol) if d == 0 else (ecol - erow), 0.0)
+                left = iota((SPAN, 128), 1) < 64
+                for p in range(2):
+                    xp = x[:, 128 * p : 128 * p + 128]
+                    nothing = jnp.zeros_like(xp)
+                    weights = [
+                        (scores * jnp.exp2((rate[d, q * 4 + 2 * p + g] * LOG2E) * gap)).astype(BF16)
+                        for g in range(2)
+                    ]
+                    yin[d, rows, 128 * p : 128 * p + 128] = mm(
+                        jnp.concatenate(weights, axis=1),
+                        jnp.concatenate(
+                            [jnp.where(left, xp, nothing), jnp.where(left, nothing, xp)], axis=0
+                        ),
+                    )
             return 0
 
         lax.fori_loop(0, halves, half, 0)
@@ -389,14 +435,16 @@
 
     xcopy(0).wait_recv()
     fcopy(0).start()
-    for k in range(1, nc):
+    last = 0
+    for k in range(nc - 1, 0, -1):
         zcopy(k).wait_recv()
         xcopy(k).start()
         pcopy(k).start()
-        complete(k - 1)
+        complete(last)
         xcopy(k).wait_recv()
         fcopy(k).start()
-    complete(nc - 1)
+        last = k
+    complete(last)
 
     for d in range(2):
         state = jnp.zeros((64, 256), F32)
@@ -448,98 +496,76 @@
         for d in range(2):
             x = proj[rows, 512 * d : 512 * d + 256]
             z = proj[rows, 512 * d + 256 : 512 * d + 512].astype(F32)
-            keys = proj[rows, 1024 + 256 * d : 1152 + 256 * d]
             queries = proj[rows, 1152 + 256 * d : 1280 + 256 * d]
-            scores = jnp.where(below if d == 0 else above, mm(queries, keys, 1, 1), 0.0)
             col = cols[d, rows, :]
             col = jnp.concatenate([col, col], axis=1)
-            row = rowv[c, d : d + 1, :]
-            gap = jnp.minimum((row - col) if d == 0 else (col - row), 0.0)
-            pairs = []
-            for p in range(2):
-                xp = x[:, 128 * p : 128 * p + 128]
-                left = iota((SPAN, 128), 1) < 64
-                nothing = jnp.zeros_like(xp)
-                weights = [
-                    (scores * jnp.exp2(rate[d, 2 * p + h] * gap)).astype(BF16) for h in range(2)
-                ]
-                pairs.append(
-                    mm(
-                        jnp.concatenate(weights, axis=1),
-                        jnp.concatenate(
-                            [jnp.where(left, xp, nothing), jnp.where(left, nothing, xp)], axis=0
-                        ),
-                    )
-                )
-            intra = jnp.concatenate(pairs, axis=1)
             lanes = rate_lane[d]
             entering = ent[d, c] + jnp.exp2(-lanes * pre[d, c][0:1]) * carried[d]
             reach = -col if d == 0 else col - ctot[c][0:1]
             inter = mm(queries[:, 0:64], entering.astype(BF16)) * jnp.exp2(lanes * reach)
-            y = dt_lane[d] * (intra + inter) + skip_lane[d] * x.astype(F32)
+            y = dt_lane[d] * (yin[d, rows, :] + inter) + skip_lane[d] * x.astype(F32)
             v = y * (z / (1.0 + jnp.exp(-z)))
             same = as_bf16((iota((256, 256), 0) // 64) == (iota((256, 256), 1) // 64))
             mean = mm((v * v).astype(BF16), same) * (1.0 / 64.0)
             normed.append((v * lax.rsqrt(mean + 1e-05)).astype(BF16))
-        terms = mm(jnp.concatenate(normed, axis=1), wo[...]).astype(BF16)
+        terms = (mm(normed[0], wo[0]) + mm(normed[1], wo[1])).astype(BF16)
         for m in range(4):
             part[m % 2, m // 2, rows, :] = terms[:, 128 * m : 128 * m + 128]
 
-    def rows_of(k):
-        return at(after(k) * slots, slots)
-
-    def acopy(k):
-        rows = rows_of(k)
-        return copy(part.at[1 - core, :, rows], recva.at[:, rows], gs.at[k], gr.at[k], to_core)
-
-    def bcopy(k):
-        rows = rows_of(k)
-        return copy(sendx.at[rows], recvx.at[rows], hs.at[k], hr.at[k], to_x)
-
-    def backcopy(k):
+    turns = list(range(nc - 1, -1, -1))
+
+    def turn(j):
+        return turns[j // halves]
+
+    def rows_of(j):
+        return at((after(turn(j)) * halves + j % halves) * SPAN, SPAN)
+
+    def acopy(j):
+        rows = rows_of(j)
+        return copy(part.at[1 - core, :, rows], recva.at[:, rows], gs.at[j], gr.at[j], to_core)
+
+    def bcopy(j):
+        rows = rows_of(j)
+        return copy(sendx.at[rows], recvx.at[rows], hs.at[j], hr.at[j], to_x)
+
+    def backcopy(j):
+        landing = at((me * halves + j % halves) * SPAN, SPAN)
         return copy(
-            sumc.at[rows_of(k)], back.at[at(me * slots, slots)], bs.at[k], br.at[k], {"curve": after(k)}
+            sumc.at[rows_of(j)], back.at[landing], bs.at[j], br.at[j], {"curve": after(turn(j))}
         )
 
-    def cross(k):
-        acopy(k).wait_recv()
-        rows = rows_of(k)
+    def cross(j):
+        acopy(j).wait_recv()
+        rows = rows_of(j)
         sendx[rows, :] = (
             part[core, 1 - xx, rows, :].astype(F32) + recva[1 - xx, rows, :].astype(F32)
         ).astype(BF16)
-        bcopy(k).start()
-
-    def home(k):
-        bcopy(k).wait_recv()
-        rows = rows_of(k)
+        bcopy(j).start()
+
+    def home(j):
+        bcopy(j).wait_recv()
+        rows = rows_of(j)
         total = (
             part[core, xx, rows, :].astype(F32)
             + recva[xx, rows, :].astype(F32)
             + recvx[rows, :].astype(F32)
         ).astype(BF16)
-        if k:
+        if turn(j):
             sumc[rows, :] = total
-            backcopy(k).start()
+            backcopy(j).start()
         else:
             back[rows, :] = total
 
-    turns = list(range(nc - 1, -1, -1))
-    for step in range(nc + 2):
-        if step < nc:
-            k = turns[step]
-
-            def one(h, _, k=k):
-                attend(after(k) * halves + h)
-                return 0
-
-            lax.fori_loop(0, halves, one, 0)
-            acopy(k).start()
-        if 1 <= step <= nc:
-            cross(turns[step - 1])
-        if 2 <= step:
-            home(turns[step - 2])
-    for k in range(1, nc):
-        backcopy(k).wait_recv()
+    for step in range(chunks + 3):
+        if step < chunks:
+            attend(after(turn(step)) * halves + step % halves)
+            acopy(step).start()
+        if 1 <= step <= chunks:
+            cross(step - 1)
+        if 3 <= step:
+            home(step - 3)
+    for j in range(chunks - halves):
+        backcopy(j).wait_recv()
     total = jnp.zeros((count, 128), F32)
     for t in range(nc):
         total = total + mm(tt[t], back[t * slots : (t + 1) * slots, :])
@@ -549,14 +575,16 @@
         xcopy(k).wait_send()
         pcopy(k).wait_send()
         fcopy(k).wait_send()
-        acopy(k).wait_send()
-        bcopy(k).wait_send()
         if k:
             zcopy(k).wait_send()
             ccopy(k).wait_send()
             scopy(k).wait_send()
             dcopy(k).wait_send()
-            backcopy(k).wait_send()
+    for j in range(chunks):
+        acopy(j).wait_send()
+        bcopy(j).wait_send()
+        if turn(j):
+            backcopy(j).wait_send()
 
 
 def fused_device(
@@ -569,34 +597,29 @@
     slots = rows // nc
     halves = slots // SPAN
     chunks = nc * halves
-    hl = HEADS // n_model
-    cut = hl * HEADDIM
-    m = lax.axis_index("mp")
-    rates = lax.dynamic_slice_in_dim(decay_rate, m * hl, hl, 1) * LOG2E
-    steps = lax.dynamic_slice_in_dim(dt_scale, m * hl, hl, 1)
-    skips = lax.dynamic_slice_in_dim(skip_gain, m * hl, hl, 1)
-    lanes = lambda a: jnp.repeat(a, HEADDIM, axis=1)[:, None, :]
-    wbc = jnp.pad(w_bc, ((0, 0), (0, 0), (0, 64))).reshape(width, 512)
-    w = jnp.concatenate([w_in.reshape(width, 4 * cut), wbc], axis=1)
-    wo = lax.dynamic_slice_in_dim(w_out, m * cut, cut, 1).reshape(2 * cut, width)
+    cut = HEADS // n_model * HEADDIM
     vm = pltpu.VMEM
     sem = pltpu.SemaphoreType.DMA
     vspec = pl.BlockSpec(memory_space=pltpu.VMEM)
+    hbm = pl.BlockSpec(memory_space=pl.ANY)
     sspec = pl.BlockSpec(memory_space=pltpu.SMEM)
     return pl.pallas_call(
         functools.partial(layer_kernel, nc, slots),
         out_shape=jax.ShapeDtypeStruct((count, width // 4), BF16),
-        in_specs=[vspec] * 8 + [sspec, vspec],
+        in_specs=[vspec] * 4 + [hbm, vspec] + [sspec] * 3 + [hbm],
         out_specs=vspec,
         scratch_shapes=[
+            vm((width, 6 * cut), BF16),
+            vm((2, cut, width), BF16),
+            sem((2,)),
             vm((nc, slots // 4, width), BF16),
             vm((nc, count, slots), BF16),
             vm((nc, halves, 8, SPAN), F32),
             vm((nc, halves, 8, SPAN), F32),
             vm((rows, width), BF16),
-            vm((rows, w.shape[1]), BF16),
+            vm((rows, 6 * cut), BF16),
             vm((2, rows, 128), F32),
-            vm((chunks, 8, SPAN), F32),
+            vm((2, rows, 256), F32),
             vm((chunks, 8, 256), F32),
             vm((2, chunks, 64, 256), F32),
             vm((2, chunks, 64, 256), F32),
@@ -613,7 +636,8 @@
             vm((rows, 128), BF16),
             vm((rows, 128), BF16),
         ]
-        + [sem((nc,))] * 20,
+        + [sem((nc,))] * 14
+        + [sem((chunks,))] * 6,
         compiler_params=pltpu.CompilerParams(
             collective_id=0, has_side_effects=True, vmem_limit_bytes=56 * 1024 * 1024
         ),
@@ -622,12 +646,12 @@
         owner.reshape(1, count),
         local_order,
         codes.reshape(1, count),
-        w,
-        lanes(rates),
-        lanes(steps),
-        lanes(skips),
-        rates,
-        wo,
+        w_in.reshape(width, 4 * cut),
+        w_bc.reshape(width, 256),
+        decay_rate,
+        dt_scale,
+        skip_gain,
+        w_out,
     )
 
 

time: 74.8 us -> 67.1 us (0.90)
  Pallas kernels: 65.7 us -> 60.9 us
  local copies, waits for them, and re-layouts: 7.57 us -> 5.9 us
  other arithmetic: 1.33 us -> 0 us
    pallas_call x1, Pallas kernels: 65.7 us -> 60.9 us  [fused_device(): pl.pallas_call(functools.partial(layer_kernel, nc, slots), out_shape=jax....]
    another operation x3 -> x0, local copies, waits for them, and re-layouts: 1.97 us -> none  [fused_device(): lanes = lambda a: jnp.repeat(a, HEADDIM, axis=1)[:, None, :]]
    reshape x1, local copies, waits for them, and re-layouts: 0.21 us -> 1.79 us  [fused_device(): w_bc.reshape(width, 256)]
    concatenate x1 -> x0, other arithmetic: 1.26 us -> none  [fused_device(): w = jnp.concatenate([w_in.reshape(width, 4 * cut), wbc], axis=1)]
    pad x1 -> x0, local copies, waits for them, and re-layouts: 1.13 us -> none  [fused_device(): wbc = jnp.pad(w_bc, ((0, 0), (0, 0), (0, 64))).reshape(width, 512)]
    unnamed x12 -> x2, local copies, waits for them, and re-layouts: 3.14 us -> 4.11 us
    dynamic_slice x2 -> x0, local copies, waits for them, and re-layouts: 0.89 us -> none  [the longest x1 0.82 us: fused_device(): lax.dynamic_slice_in_dim(w_out, m * cut, cut, 1).reshape(2 * cut, width)]
where the time goes in v1:
time: 67.1 us; the launch traced here: 66.8 us
  Pallas kernels  60.9 us (91%)
  local copies, waits for them, and re-layouts  5.9 us (9%)
    pallas_call x1, Pallas kernels, fused_device(): pl.pallas_call(functools.partial(layer_kernel, nc, slots), out_shape=jax....  60.9 us
    unnamed x2, local copies, waits for them, and re-layouts  4.11 us
    reshape x1, local copies, waits for them, and re-layouts, fused_device(): w_bc.reshape(width, 256)  1.79 us

profile of v1, /device:TPU:0, one launch (start us, length us, event | category | flops | bytes accessed | tf_op | source)
XLA Modules:
  0.0 66.8 jit_solution(12840319796661242821)
XLA Ops:
  0.0 1.8 %copy.12.w_bc = bf16[512,256]{1,0:T(8,128)(2,1)} copy(bf16[512,256]{0,1:T(8,128)(2,1)} %bitcast.7) | data formatting | bytes 524288 | tf_op jit(solution)/shard_map/reshape | solution.py:650
  1.8 2.4 %copy.13 = bf16[64,8,4,256]{3,1,2,0:T(8,128)(2,1)} copy(bf16[64,8,4,256]{3,2,1,0:T(4,128)(2,1)} %bitcast.6) | data formatting | bytes 2097152
  4.2 60.9 %shard_map.100 = bf16[1024,128]{1,0:T(8,128)(2,1)} custom-call(bf16[1024,512]{1,0:T(8,128)(2,1)} %pts.1, s32[1,1024]{1,0:T(1,128)} %bitcast.8, s32[1,1024]{1,0:T(1,128)} %order.1, s32[1,1024]{1,0:T(1,128)} %bitcast.9, bf16[512,1024]{1,0:T(8,128)(2,1)} %bitcast.5, bf16[512,256]{1,0:T(8,128)(2,1)} %copy.12.w_bc, f32[2,16]{1,0:T(2,128)} %rate.1, f32[2,16]{1,0:T(2,128)} %dt.1, ...), custom_call_target="tpu_custom_call" | custom-call | tf_op jit(solution)/shard_map/pallas_call | solution.py:606
  65.2 1.7 %copy.15 = bf16[1024,128]{1,0:T(8,128)(2,1)} copy(bf16[1024,128]{1,0:T(8,128)(2,1)} %shard_map.100) | data formatting | bytes 524288

commit v2 on v1

--- a/solution.py
+++ b/solution.py
@@ -300,8 +300,16 @@
     own8 = jnp.broadcast_to(own[...].astype(F32), (8, count)).astype(BF16)
     sorted8 = mm(own8, picks)
     hot8 = as_bf16(sorted8 == iota((8, count), 0).astype(F32))
-    upper = as_bf16(iota((count, count), 0) <= iota((count, count), 1))
-    counts = mm(hot8, upper)
+    upper = as_bf16(iota((128, 128), 0) <= iota((128, 128), 1))
+    stripes = range(count // 128)
+    runs = mm(jnp.concatenate([hot8[:, 128 * b : 128 * b + 128] for b in stripes], axis=0), upper)
+    base = jnp.zeros((8, 1), F32)
+    pieces = []
+    for b in stripes:
+        run = runs[8 * b : 8 * b + 8]
+        pieces.append(run + base)
+        base = base + run[:, 127:128]
+    counts = jnp.concatenate(pieces, axis=1)
     slot = jnp.sum(counts * hot8.astype(F32), axis=0, keepdims=True) - 1.0
     target = sorted8[0:1] * float(slots) + slot
     high = jnp.floor(target * (1.0 / 64.0))
@@ -309,8 +317,6 @@
     split8 = jnp.where(iota((8, count), 0) == 0, high, low).astype(BF16)
     trow8 = mm(split8, picks, 1, 1)
     trow = trow8[0:1] * 64.0 + trow8[1:2]
-    tcol8 = mm(picks, split8, 1, 1)
-    tcol = tcol8[:, 0:1] * 64.0 + tcol8[:, 1:2]
 
     def routed(t):
         place = (iota((share, count), 0) + (t * slots + q * share)).astype(F32)
@@ -354,6 +360,8 @@
     xcopy(0).start()
     pcopy(0).start()
 
+    tcol8 = mm(picks, split8, 1, 1)
+    tcol = tcol8[:, 0:1] * 64.0 + tcol8[:, 1:2]
     codef = codes[...].astype(F32)
     chigh = jnp.floor(codef * (1.0 / 128.0))
     code8 = jnp.where(iota((8, count), 0) == 0, chigh, codef - chigh * 128.0).astype(BF16)
@@ -412,16 +420,22 @@
                 for p in range(2):
                     xp = x[:, 128 * p : 128 * p + 128]
                     nothing = jnp.zeros_like(xp)
-                    weights = [
-                        (scores * jnp.exp2((rate[d, q * 4 + 2 * p + g] * LOG2E) * gap)).astype(BF16)
-                        for g in range(2)
-                    ]
-                    yin[d, rows, 128 * p : 128 * p + 128] = mm(
-                        jnp.concatenate(weights, axis=1),
-                        jnp.concatenate(
-                            [jnp.where(left, xp, nothing), jnp.where(left, nothing, xp)], axis=0
-                        ),
-                    )
+                    lower_x = jnp.where(left, xp, nothing)
+                    upper_x = jnp.where(left, nothing, xp)
+                    for r in range(2):
+                        lo, hi = (0, 128 * r + 128) if d == 0 else (128 * r, 256)
+                        top = slice(128 * r, 128 * r + 128)
+                        weights = [
+                            (
+                                scores[top, lo:hi]
+                                * jnp.exp2((rate[d, q * 4 + 2 * p + g] * LOG2E) * gap[top, lo:hi])
+                            ).astype(BF16)
+                            for g in range(2)
+                        ]
+                        yin[d, at(c * SPAN + 128 * r, 128), 128 * p : 128 * p + 128] = mm(
+                            jnp.concatenate(weights, axis=1),
+                            jnp.concatenate([lower_x[lo:hi], upper_x[lo:hi]], axis=0),
+                        )
             return 0
 
         lax.fori_loop(0, halves, half, 0)

time: 67.1 us -> 65.2 us (0.972)
  Pallas kernels: 60.9 us -> 59 us
    pallas_call x1, Pallas kernels: 60.9 us -> 59 us  [fused_device(): pl.pallas_call(functools.partial(layer_kernel, nc, slots), out_shape=jax....]
where the time goes in v2:
time: 65.2 us; the launch traced here: 64.9 us
  Pallas kernels  59 us (90%)
  local copies, waits for them, and re-layouts  5.9 us (9%)
    pallas_call x1, Pallas kernels, fused_device(): pl.pallas_call(functools.partial(layer_kernel, nc, slots), out_shape=jax....  59 us
    unnamed x2, local copies, waits for them, and re-layouts  4.11 us
    reshape x1, local copies, waits for them, and re-layouts, fused_device(): w_bc.reshape(width, 256)  1.79 us

profile of v2, /device:TPU:0, one launch (start us, length us, event | category | flops | bytes accessed | tf_op | source)
XLA Modules:
  0.0 64.9 jit_solution(4256949777728210738)
XLA Ops:
  0.0 1.8 %copy.12.w_bc = bf16[512,256]{1,0:T(8,128)(2,1)} copy(bf16[512,256]{0,1:T(8,128)(2,1)} %bitcast.7) | data formatting | bytes 524288 | tf_op jit(solution)/shard_map/reshape | solution.py:664
  1.8 2.4 %copy.13 = bf16[64,8,4,256]{3,1,2,0:T(8,128)(2,1)} copy(bf16[64,8,4,256]{3,2,1,0:T(4,128)(2,1)} %bitcast.6) | data formatting | bytes 2097152
  4.2 59.0 %shard_map.100 = bf16[1024,128]{1,0:T(8,128)(2,1)} custom-call(bf16[1024,512]{1,0:T(8,128)(2,1)} %pts.1, s32[1,1024]{1,0:T(1,128)} %bitcast.8, s32[1,1024]{1,0:T(1,128)} %order.1, s32[1,1024]{1,0:T(1,128)} %bitcast.9, bf16[512,1024]{1,0:T(8,128)(2,1)} %bitcast.5, bf16[512,256]{1,0:T(8,128)(2,1)} %copy.12.w_bc, f32[2,16]{1,0:T(2,128)} %rate.1, f32[2,16]{1,0:T(2,128)} %dt.1, ...), custom_call_target="tpu_custom_call" | custom-call | tf_op jit(solution)/shard_map/pallas_call | solution.py:620
  63.3 1.7 %copy.15 = bf16[1024,128]{1,0:T(8,128)(2,1)} copy(bf16[1024,128]{1,0:T(8,128)(2,1)} %shard_map.100) | data formatting | bytes 524288
